TPU v7x, 32 devices: a whole 2x2x4 slice. The times are simulated.
32 devices in a mesh: seq: 8 (over z, x), tensor: 4 (over y, core).
Axes of the slice: x: 2, y: 2, z: 4, core: 2. Of those that a mesh axis runs over, the one named last changes fastest.
Arguments:
- hidden_in: bfloat16 [1024, 4096], P(('seq', 'tensor')), may hold values from -30 to 30
- prev_amax: float32 [], replicated, may hold values from 5 to 9
- w_x: bfloat16 [4096, 8192], P('seq', 'tensor'), may hold values from -0.09375 to 0.09375
- w_bc: bfloat16 [4096, 8, 2, 128], P('seq', 'tensor'), may hold values from -0.046875 to 0.046875
- w_dt: bfloat16 [4096, 128], P('seq', 'tensor'), may hold values from -0.09375 to 0.09375
- conv_x: float32 [4, 8192], P(None, 'tensor'), may hold values from -4 to 4
- conv_bc: float32 [4, 8, 2, 128], P(None, 'tensor'), may hold values from -4 to 4
- conv_state_x: bfloat16 [3, 8192], P(None, 'tensor'), may hold values from -6 to 6
- conv_state_bc: bfloat16 [3, 8, 2, 128], P(None, 'tensor'), may hold values from -3 to 3
- dt_bias: float32 [128], P('tensor'), may hold values from -2 to 1
- decay_rate: float32 [128], P('tensor'), may hold values from 9.765625e-05 to 0.12
- skip: float32 [128], P('tensor'), may hold values from 0.5 to 4
- init_state: float32 [128, 64, 128], P('tensor'), may hold values from -48 to 48
- norm_gain: float32 [8192], P('tensor'), may hold values from 0.1 to 1.9
- w_out: bfloat16 [8192, 4096], P('tensor', 'seq'), may hold values from -0.0625 to 0.0625
Outputs:
- layer_out: bfloat16 [1024, 4096], P(('seq', 'tensor'))
- abs_max: float32 [], replicated
All inputs are finite; a program needn't handle non-finite values.
Results may differ from a plain program's by a relative error of at most 0.019.
Values may be sent and summed in bfloat16 or wider, within the bound.
No kernel may reach another device: no remote copies, remote signals or barrier semaphores. Data moves between devices by JAX's collectives and lax.ppermute only.
A program may use at most 64 MiB of HBM per device.

v0:
```python
import jax
import jax.numpy as jnp
from jax import lax
from jax.sharding import PartitionSpec as P

HEADS = 128
HEAD_DIM = 64
STATE = 128
GROUPS = 8
KERNEL = 4
SPAN = 128


epsilon = 1e-05
quant_range = 448.0


def from_behind(value, axis, steps):
    count = lax.axis_size(axis)
    first, last = (max(0, -steps), min(count, count - steps))
    return lax.ppermute(value, axis, [(source, source + steps) for source in range(first, last)])


def carried_in(shard, axis, combine, identity):
    count, here = (lax.axis_size(axis), lax.axis_index(axis))
    everything = jax.tree.map(
        lambda part, kind: lax.all_gather(part.astype(kind), axis),
        shard,
        (jnp.bfloat16, jnp.bfloat16),
    )
    start = jax.tree.map(
        lambda part, zero: jnp.broadcast_to(jnp.asarray(zero, part.dtype), part.shape),
        shard,
        identity,
    )

    def turn(k, before):
        reached = k < here
        new = combine(
            before, jax.tree.map(lambda part, own: part[k].astype(own.dtype), everything, shard)
        )
        return jax.tree.map(lambda a, b: jnp.where(reached, a, b), new, before)

    return lax.fori_loop(0, count, turn, start)


def depthwise(before, projected, conv_taps, length):
    extended = jnp.concatenate([before, projected], axis=0)
    summed = conv_taps[0] * extended[0:length]
    for offset in range(1, KERNEL):
        summed = summed + conv_taps[offset] * extended[offset : offset + length]
    return jax.nn.silu(summed).astype(jnp.bfloat16)


def combine(earlier, later):
    return (earlier[0] * later[0], later[0][:, None, None] * earlier[1] + later[1])


def local(
    hidden_in,
    prev_amax,
    w_x,
    w_bc,
    w_dt,
    conv_x,
    conv_bc,
    conv_state_x,
    conv_state_bc,
    dt_bias,
    decay_rate,
    skip,
    init_state,
    norm_gain,
    w_out,
):
    margin = KERNEL - 1
    gathered = lax.all_gather(hidden_in, "tensor", axis=0, tiled=True)
    abs_max = lax.pmax(jnp.max(jnp.abs(gathered.astype(jnp.float32))), "seq")
    in_scale = prev_amax / quant_range
    leading = lax.axis_index("seq") == 0
    row_count = gathered.shape[0]
    bc_width = w_bc.shape[1] * w_bc.shape[2] * w_bc.shape[3]
    bc_rows = jnp.reshape(w_bc, (w_bc.shape[0], bc_width))
    scaled = gathered.astype(jnp.float32) * (quant_range / prev_amax)
    quant = jnp.clip(scaled, -quant_range, quant_range).astype(jnp.bfloat16)
    pieces = (
        lax.all_gather(w_x, "seq", axis=0, tiled=True),
        lax.all_gather(bc_rows, "seq", axis=0, tiled=True),
        lax.all_gather(w_dt, "seq", axis=0, tiled=True),
    )
    x_proj, bc_proj, dt_proj = tuple(
        (
            jnp.dot(quant, weight_piece, preferred_element_type=jnp.float32)
            for weight_piece in pieces
        )
    )
    x_whole = (x_proj * in_scale).astype(jnp.bfloat16)
    bc_whole = (bc_proj * in_scale).astype(jnp.bfloat16)
    dt_raw = dt_proj * in_scale
    state_bc = jnp.reshape(conv_state_bc, (margin, bc_width))
    received = from_behind(
        (x_whole[row_count - margin :], bc_whole[row_count - margin :]), "seq", 1
    )
    x_edge = jnp.where(leading, conv_state_x, received[0])
    bc_edge = jnp.where(leading, state_bc, received[1])
    x_act = depthwise(x_edge, x_whole, conv_x, row_count)
    bc_act = depthwise(bc_edge, bc_whole, jnp.reshape(conv_bc, (KERNEL, bc_width)), row_count)
    step_size = jax.nn.softplus(dt_raw + dt_bias)
    heads_here = step_size.shape[1]
    groups_here = w_bc.shape[1]
    per_group = HEADS // GROUPS
    blocks = row_count // SPAN
    x_blocks = x_act.reshape(blocks, SPAN, heads_here, HEAD_DIM)
    bc_blocks = bc_act.reshape(blocks, SPAN, groups_here, 2, STATE)
    in_map = bc_blocks[:, :, :, 0]
    out_map = bc_blocks[:, :, :, 1]
    step_blocks = step_size.reshape(blocks, SPAN, heads_here)
    cum_blocks = jnp.cumsum(-step_blocks * decay_rate, axis=1)
    index_row = jnp.arange(SPAN, dtype=jnp.int32)
    lower_mask = index_row[:, None] >= index_row[None, :]
    intersection = jnp.einsum(
        "ctgn,cugn->cgtu", out_map, in_map, preferred_element_type=jnp.float32
    )
    intersection = jnp.repeat(intersection, per_group, axis=1)
    cum_heads = jnp.transpose(cum_blocks, (0, 2, 1))
    log_gap = cum_heads[:, :, :, None] - cum_heads[:, :, None, :]
    decay = jnp.exp(jnp.where(lower_mask[None, None], log_gap, -1e30))
    step_heads = jnp.transpose(step_blocks, (0, 2, 1))
    weights = (intersection * decay * step_heads[:, :, None, :]).astype(jnp.bfloat16)
    local_part = jnp.einsum(
        "chtu,cuhp->cthp", weights, x_blocks, preferred_element_type=jnp.float32
    )
    last_cum = cum_blocks[:, SPAN - 1, :]
    x_weighted = (
        x_blocks.astype(jnp.float32)
        * (step_blocks * jnp.exp(last_cum[:, None, :] - cum_blocks))[:, :, :, None]
    ).astype(jnp.bfloat16)
    in_heads = jnp.repeat(in_map, per_group, axis=2)
    added = jnp.einsum("cuhp,cuhn->chpn", x_weighted, in_heads, preferred_element_type=jnp.float32)

    def carry_on(carried, element):
        block_decay, block_added = element
        return (block_decay[:, None, None] * carried + block_added, carried)

    empty_state = jnp.zeros((heads_here, HEAD_DIM, STATE), jnp.float32)
    device_state, entering = lax.scan(carry_on, empty_state, (jnp.exp(last_cum), added))
    device_decay = jnp.exp(jnp.sum(last_cum, axis=0))
    seeded = device_state + jnp.where(leading, device_decay[:, None, None] * init_state, 0.0)
    identity = (jnp.ones_like(device_decay), jnp.zeros_like(device_state))
    scanned = carried_in((device_decay, seeded), "seq", combine, identity)
    incoming = jnp.where(leading, init_state, scanned[1])
    prefix = jnp.exp(jnp.cumsum(last_cum, axis=0) - last_cum)
    states_in = entering + prefix[:, :, None, None] * incoming[None]
    out_heads = jnp.repeat(out_map, per_group, axis=2).astype(jnp.float32)
    carried_part = (
        jnp.einsum("cthn,chpn->cthp", out_heads, states_in, precision=lax.Precision.HIGHEST)
        * jnp.exp(cum_blocks)[:, :, :, None]
    )
    ssm_out = local_part + carried_part + skip[None, None, :, None] * x_blocks.astype(jnp.float32)
    ssm_out = ssm_out.reshape(row_count, heads_here * HEAD_DIM)
    squares = lax.psum(jnp.sum(ssm_out * ssm_out, axis=1), "tensor")
    mean_sq = squares / (HEADS * HEAD_DIM)
    normed = (ssm_out * lax.rsqrt(mean_sq + epsilon)[:, None] * norm_gain).astype(jnp.bfloat16)
    partial_out = jnp.dot(
        normed, lax.all_gather(w_out, "seq", axis=1, tiled=True), preferred_element_type=jnp.float32
    )
    layer_out = lax.psum_scatter(
        partial_out.astype(jnp.bfloat16), "tensor", scatter_dimension=0, tiled=True
    )
    return (layer_out, abs_max)


def solution(mesh):
    return jax.shard_map(
        local,
        mesh=mesh,
        in_specs=(
            P(("seq", "tensor"), None),
            P(),
            P("seq", "tensor"),
            P("seq", "tensor", None, None),
            P("seq", "tensor"),
            P(None, "tensor"),
            P(None, "tensor", None, None),
            P(None, "tensor"),
            P(None, "tensor", None, None),
            P("tensor"),
            P("tensor"),
            P("tensor"),
            P("tensor", None, None),
            P("tensor"),
            P("tensor", "seq"),
        ),
        out_specs=(P(("seq", "tensor"), None), P()),
        check_vma=False,
    )
```

profile of v0, /device:TPU:0, one launch (start us, length us, event | category | flops | bytes accessed | tf_op | source)
XLA Modules:
  0.0 689.0 jit_solution(9792995852269013818)
XLA Ops:
  8.0 2.0 reshape.205
  11.6 32.7 %all_gather.28 = bf16[4096,32]{0,1:T(8,128)(2,1)S(1)} all-gather(bf16[512,32]{0,1:T(8,128)(2,1)S(1)} %copy-done.3), channel_id=1, replica_groups=mesh['seq'=8,'tensor'=4] {'seq'}, dimensions={0}, use_global_device_ids=true | all-gather | bytes 294912 | tf_op jit(solution)/shard_map/all_gather | solution.py:89
  44.3 1.8 compare_select_fusion
  46.6 58.1 %all-gather.12.cloned.1.call-done = bf16[4096,512]{1,0:T(8,128)(2,1)} async-done(((bf16[512,512]{1,0:T(8,128)(2,1)}), bf16[4096,512]{1,0:T(8,128)(2,1)}) %all-gather.12.cloned.1.call-update) | async-done | bytes 4194320 | tf_op jit(solution)/shard_map/all_gather | solution.py:88
  104.7 2.9 fusion.12
  107.6 2.5 collective-permute-start.1
  110.1 1.3 collective-permute-done.1
  111.9 220.9 %all-gather.10.cloned.1.call-done = bf16[4096,2048]{1,0:T(8,128)(2,1)} async-done(((bf16[512,2048]{1,0:T(8,128)(2,1)}), bf16[4096,2048]{1,0:T(8,128)(2,1)}) %all-gather.10.cloned.1.call-update) | async-done | bytes 16777232 | tf_op jit(solution)/shard_map/all_gather | solution.py:87
  332.7 8.1 %fusion.1 = bf16[128,2048]{1,0:T(8,128)(2,1)S(1)} fusion(bf16[4096,2048]{1,0:T(8,128)(2,1)} %all-gather.10.cloned.1.call-done, bf16[128,4096]{1,0:T(8,128)(2,1)S(1)} %copy-done, f32[]{:T(128)S(6)} %div.20, f32[]{:T(128)S(6)} %div.21), kind=kOutput, calls=%fused_computation.7 | convolution fusion | flops 2150105088 | bytes 18350088 | tf_op jit(solution)/shard_map/dot_general | solution.py:93
  340.9 2.6 collective-permute-start
  343.5 1.4 collective-permute-done
  346.2 1.2 fusion.11
  348.1 19.3 %all-gather = bf16[8,1,32]{2,1,0:T(2,128)(2,1)S(1)} all-gather(bf16[1,1,32]{2,1,0:T(2,128)(2,1)S(1)} %get-tuple-element.146), channel_id=2, replica_groups=mesh['seq'=8,'tensor'=4] {'seq'}, dimensions={0}, use_global_device_ids=true | all-gather | bytes 576 | tf_op jit(solution)/shard_map/all_gather | solution.py:27
  367.6 1.5 fusion.6
  370.3 3.0 convolution_bitcast_fusion.1
  373.4 48.4 %all-gather.16.cloned.1.call-done = bf16[256,64,128]{2,1,0:T(8,128)(2,1)} async-done(((bf16[32,64,128]{2,1,0:T(8,128)(2,1)}), bf16[256,64,128]{2,1,0:T(8,128)(2,1)}) %all-gather.16.cloned.1.call-update) | async-done | bytes 4194320 | tf_op jit(solution)/shard_map/all_gather | solution.py:27
  421.8 11.1 %while.9 = (s32[]{:T(128)}, f32[32,64,128]{2,1,0:T(8,128)S(1)}, s32[]{:T(128)}, bf16[8,32]{1,0:T(8,128)(2,1)S(1)}, bf16[8,32,64,128]{3,2,1,0:T(8,128)(2,1)}, /*index=5*/s32[]{:T(128)}, s32[]{:T(128)}) while((s32[]{:T(128)}, f32[32,64,128]{2,1,0:T(8,128)S(1)}, s32[]{:T(128)}, bf16[8,32]{1,0:T(8,128)(2,1)S(1)}, ...), condition=%wide.region_2.3_spmd.clone, body=%wide.region_1.0_spmd.clone.sunk | while | flops 1310756 | bytes 2621873 | solution.py:44
  421.8 1.4 fusion.55
  423.2 1.3 fusion.55
  424.6 1.3 fusion.55
  425.9 1.3 fusion.55
  427.3 1.3 fusion.55
  428.6 1.4 fusion.55
  430.0 1.4 fusion.55
  431.5 1.4 fusion.55
  433.1 4.8 multiply_reduce_fusion
  438.0 6.2 psum.7
  444.2 1.6 fusion.15
  445.8 204.0 %all-gather.14.cloned.1.call-done = bf16[2048,4096]{1,0:T(8,128)(2,1)} async-done(((bf16[2048,512]{1,0:T(8,128)(2,1)}), bf16[2048,4096]{1,0:T(8,128)(2,1)}) %all-gather.14.cloned.1.call-update) | async-done | bytes 16777232 | tf_op jit(solution)/shard_map/all_gather | solution.py:165
  649.7 9.1 %convolution_convert_fusion = bf16[128,4096]{1,0:T(8,128)(2,1)} fusion(bf16[128,2048]{0,1:T(8,128)(2,1)S(1)} %fusion.15, bf16[2048,4096]{1,0:T(8,128)(2,1)} %all-gather.14.cloned.1.call-done), kind=kOutput, calls=%fused_computation.3 | convolution fusion | flops 2148007936 | bytes 18350080 | tf_op jit(solution)/shard_map/dot_general | solution.py:164
  659.6 19.2 %pmax.7 = f32[]{:T(128)} all-reduce(f32[]{:T(128)} %fusion.4), channel_id=1, replica_groups=mesh['seq'=8,'tensor'=4] {'seq'}, use_global_device_ids=true, to_apply=%region_7.8 | all-reduce | flops 1 | bytes 8 | tf_op jit(solution)/shard_map/pmax | solution.py:78
  678.8 3.3 reduce-scatter.2.cloned.1.call-done
  (75 shorter events, 6.9 us)
Async XLA Ops:
  7.2 4.4 copy-start.8
  7.2 4.4 copy-start.3
  7.2 37.1 %copy-start.7 = (f32[4,2,2,128]{3,2,1,0:T(2,128)S(1)}, f32[4,2,2,128]{3,2,1,0:T(2,128)}, u32[]{:S(2)}) copy-start(f32[4,2,2,128]{3,2,1,0:T(2,128)} %param.23) | copy-start | bytes 24580
  7.2 37.0 %copy-start.4 = (f32[4,2048]{1,0:T(4,128)S(1)}, f32[4,2048]{1,0:T(4,128)}, u32[]{:S(2)}) copy-start(f32[4,2048]{1,0:T(4,128)} %param.22) | copy-start | bytes 98308
  7.2 37.1 %all-gather.8.cloned.1.call-start = ((), (), s32[]{:S(2)}) async-start(), calls=%async_computation.1 | async-start | bytes 1310720 | tf_op jit(solution)/shard_map/all_gather | solution.py:77
  7.9 36.4 %copy-start.11 = (f32[32]{0:T(128)S(1)}, f32[32]{0:T(128)}, u32[]{:S(2)}) copy-start(f32[32]{0:T(128)} %param.26) | copy-start | bytes 388
  7.9 96.8 %all-gather.12.cloned.1.call-start = ((), (), s32[]{:S(2)}) async-start(), calls=%async_computation.3 | async-start | bytes 4718592 | tf_op jit(solution)/shard_map/all_gather | solution.py:88
  10.1 36.1 %copy-start.9 = (f32[32]{0:T(128)S(1)}, f32[32]{0:T(128)}, u32[]{:S(2)}) copy-start(f32[32]{0:T(128)} %param.27) | copy-start | bytes 388
  10.1 322.7 %all-gather.10.cloned.1.call-start = ((), (), s32[]{:S(2)}) async-start(), calls=%async_computation.2 | async-start | bytes 18874368 | tf_op jit(solution)/shard_map/all_gather | solution.py:87
  10.8 411.0 %all-gather.16.cloned.1.call-start = ((), (), s32[]{:S(2)}) async-start(), calls=%async_computation.6 | async-start | bytes 4718592 | tf_op jit(solution)/shard_map/all_gather | solution.py:27
  44.3 60.4 %copy-start = (bf16[128,4096]{1,0:T(8,128)(2,1)S(1)}, bf16[128,4096]{1,0:T(8,128)(2,1)}, u32[]{:S(2)}) copy-start(bf16[128,4096]{1,0:T(8,128)(2,1)} %all-gather.8.cloned.1.call-done) | copy-start | bytes 3145732
  107.6 3.8 collective-permute-start.1
  111.8 233.1 %copy-start.5 = (bf16[3,2048]{1,0:T(4,128)(2,1)S(1)}, bf16[3,2048]{1,0:T(4,128)(2,1)}, u32[]{:S(2)}) copy-start(bf16[3,2048]{1,0:T(4,128)(2,1)} %param.24) | copy-start | bytes 36868
  340.9 5.3 copy-start.1
  340.9 4.0 collective-permute-start
  347.4 302.3 %all-gather.14.cloned.1.call-start = ((), (), s32[]{:S(2)}) async-start(), calls=%async_computation.4 | async-start | bytes 18874368 | tf_op jit(solution)/shard_map/all_gather | solution.py:165
  348.0 334.1 %reduce-scatter.2.cloned.1.call-start = ((), (), s32[]{:S(2)}) async-start(), calls=%async_computation.5 | async-start | bytes 1310720 | tf_op jit(solution)/shard_map/reduce_scatter | solution.py:167
  421.8 11.3 %copy-start.2 = (f32[32,64,128]{2,1,0:T(8,128)S(1)}, f32[32,64,128]{2,1,0:T(8,128)}, u32[]{:S(2)}) copy-start(f32[32,64,128]{2,1,0:T(8,128)} %param.29) | copy-start | bytes 3145732
  421.8 11.3 %copy-start.10 = (f32[32]{0:T(128)S(1)}, f32[32]{0:T(128)}, u32[]{:S(2)}) copy-start(f32[32]{0:T(128)} %param.28) | copy-start | bytes 388
  433.1 11.1 %copy-start.6 = (f32[2048]{0:T(1024)S(1)}, f32[2048]{0:T(1024)}, u32[]{:S(2)}) copy-start(f32[2048]{0:T(1024)} %param.30) | copy-start | bytes 24580
Sparse Core Ops, SparseCore 0:
  9.6 19.4 all-gather.7
  31.2 73.4 all-gather.11
  106.8 225.8 all-gather.9
  347.5 74.2 all-gather.15
  423.7 226.0 all-gather.13
  659.0 23.0 reduce-scatter.1
where the time goes:
time: 690 us; the launch traced here: 689 us
  waiting for transfers between devices  539 us (78%)
  blocking collectives  77.4 us (11%)
  matrix products  31.1 us (5%)
  other arithmetic  15.9 us (2%)
  between operations  15.1 us (2%)
    all_gather x1, waiting for transfers between devices, local(): lax.all_gather(w_x, 'seq', axis=0, tiled=True)  221 us
    all_gather x1, waiting for transfers between devices, local(): lax.all_gather(w_out, 'seq', axis=1, tiled=True)  204 us
    all_gather x1, waiting for transfers between devices, local(): lax.all_gather(bc_rows, 'seq', axis=0, tiled=True)  58.1 us
    all_gather x1, waiting for transfers between devices, carried_in(): lax.all_gather(part.astype(kind), axis)  48.4 us
    all_gather x1, blocking collectives, local(): lax.all_gather(w_dt, 'seq', axis=0, tiled=True)  32.7 us
    all_gather x1, blocking collectives, carried_in(): lax.all_gather(part.astype(kind), axis)  19.3 us
    pmax x1, blocking collectives, local(): abs_max = lax.pmax(jnp.max(jnp.abs(gathered.astype(jnp.float32))), 'seq')  19.2 us
  transfers between devices with their start and end apart: 8, of which 7 were waited for; matrix products, arithmetic and copies ran while one was open for 5% of the time, Pallas kernels for 0%

commit v1 on v0

--- a/solution.py
+++ b/solution.py
@@ -56,7 +56,7 @@
     return (earlier[0] * later[0], later[0][:, None, None] * earlier[1] + later[1])
 
 
-def local(
+def by_tokens(
     hidden_in,
     prev_amax,
     w_x,
@@ -170,9 +170,141 @@
     return (layer_out, abs_max)
 
 
+def project(weight, quant, in_scale):
+    return jnp.dot(quant, weight, preferred_element_type=jnp.float32) * in_scale
+
+
+def by_heads(
+    hidden_in,
+    prev_amax,
+    w_x,
+    w_bc,
+    w_dt,
+    conv_x,
+    conv_bc,
+    conv_state_x,
+    conv_state_bc,
+    dt_bias,
+    decay_rate,
+    skip,
+    init_state,
+    norm_gain,
+    w_out,
+):
+    margin = KERNEL - 1
+    count, here = (lax.axis_size("seq"), lax.axis_index("seq"))
+    abs_max = lax.pmax(jnp.max(jnp.abs(hidden_in.astype(jnp.float32))), ("seq", "tensor"))
+    in_scale = prev_amax / quant_range
+    scaled = hidden_in.astype(jnp.float32) * (quant_range / prev_amax)
+    quant_rows = jnp.clip(scaled, -quant_range, quant_range).astype(jnp.bfloat16)
+    depth = w_x.shape[0]
+    own = hidden_in.shape[0]
+    ranks = lax.axis_size("tensor")
+    pieces = quant_rows.reshape(own, count, depth).transpose(1, 0, 2)
+    mine = lax.all_to_all(pieces, "seq", split_axis=0, concat_axis=0, tiled=True)
+    rows = lax.all_gather(mine, "tensor", axis=1)
+    tokens = count * ranks * own
+    quant = rows.reshape(tokens, depth)
+    bc_width = w_bc.shape[1] * w_bc.shape[2] * w_bc.shape[3]
+    channels = w_x.shape[1] // count
+    heads_all = w_dt.shape[1]
+    heads_here = heads_all // count
+    groups_here = w_bc.shape[1]
+    sharing = count // groups_here
+    x_part = jnp.stack(
+        [
+            project(w_x[:, k * channels : (k + 1) * channels], quant, in_scale)
+            for k in range(count)
+        ]
+    ).astype(jnp.bfloat16)
+    x_pre = lax.psum_scatter(x_part, "seq", scatter_dimension=0, tiled=True)[0]
+    bc_part = project(w_bc.reshape(depth, bc_width), quant, in_scale).astype(jnp.bfloat16)
+    bc_pre = lax.psum(bc_part, "seq")
+    dt_part = project(w_dt, quant, in_scale)
+    dt_raw = lax.psum(dt_part, "seq")
+    group = here // sharing
+    group_width = 2 * STATE
+    bc_mine = lax.dynamic_slice_in_dim(bc_pre, group * group_width, group_width, axis=1)
+    dt_mine = lax.dynamic_slice_in_dim(dt_raw, here * heads_here, heads_here, axis=1)
+    channel_at = here * channels
+    head_at = here * heads_here
+    x_edge = lax.dynamic_slice_in_dim(conv_state_x, channel_at, channels, axis=1)
+    x_taps = lax.dynamic_slice_in_dim(conv_x, channel_at, channels, axis=1)
+    bc_edge = lax.dynamic_slice_in_dim(
+        conv_state_bc.reshape(margin, bc_width), group * group_width, group_width, axis=1
+    )
+    bc_taps = lax.dynamic_slice_in_dim(
+        conv_bc.reshape(KERNEL, bc_width), group * group_width, group_width, axis=1
+    )
+    x_act = depthwise(x_edge, x_pre, x_taps, tokens)
+    bc_act = depthwise(bc_edge, bc_mine, bc_taps, tokens)
+    bias = lax.dynamic_slice_in_dim(dt_bias, head_at, heads_here)
+    rate = lax.dynamic_slice_in_dim(decay_rate, head_at, heads_here)
+    skips = lax.dynamic_slice_in_dim(skip, head_at, heads_here)
+    start = lax.dynamic_slice_in_dim(init_state, head_at, heads_here, axis=0)
+    step_size = jax.nn.softplus(dt_mine + bias)
+    blocks = tokens // SPAN
+    x_blocks = x_act.reshape(blocks, SPAN, heads_here, HEAD_DIM)
+    in_map = bc_act[:, :STATE].reshape(blocks, SPAN, STATE)
+    out_map = bc_act[:, STATE:].reshape(blocks, SPAN, STATE)
+    step_blocks = step_size.reshape(blocks, SPAN, heads_here)
+    cum_blocks = jnp.cumsum(-step_blocks * rate, axis=1)
+    index_row = jnp.arange(SPAN, dtype=jnp.int32)
+    lower_mask = index_row[:, None] >= index_row[None, :]
+    intersection = jnp.einsum("ctn,cun->ctu", out_map, in_map, preferred_element_type=jnp.float32)
+    cum_heads = jnp.transpose(cum_blocks, (0, 2, 1))
+    log_gap = cum_heads[:, :, :, None] - cum_heads[:, :, None, :]
+    decay = jnp.exp(jnp.where(lower_mask[None, None], log_gap, -1e30))
+    step_heads = jnp.transpose(step_blocks, (0, 2, 1))
+    weights = (intersection[:, None] * decay * step_heads[:, :, None, :]).astype(jnp.bfloat16)
+    local_part = jnp.einsum("chtu,cuhp->cthp", weights, x_blocks, preferred_element_type=jnp.float32)
+    last_cum = cum_blocks[:, SPAN - 1, :]
+    x_weighted = (
+        x_blocks.astype(jnp.float32)
+        * (step_blocks * jnp.exp(last_cum[:, None, :] - cum_blocks))[:, :, :, None]
+    ).astype(jnp.bfloat16)
+    added = jnp.einsum("cuhp,cun->chpn", x_weighted, in_map, preferred_element_type=jnp.float32)
+
+    def carry_on(carried, element):
+        block_decay, block_added = element
+        return (block_decay[:, None, None] * carried + block_added, carried)
+
+    unused, states_in = lax.scan(carry_on, start, (jnp.exp(last_cum), added))
+    carried_part = (
+        jnp.einsum(
+            "ctn,chpn->cthp", out_map.astype(jnp.float32), states_in, precision=lax.Precision.HIGHEST
+        )
+        * jnp.exp(cum_blocks)[:, :, :, None]
+    )
+    ssm_out = local_part + carried_part + skips[None, None, :, None] * x_blocks.astype(jnp.float32)
+    ssm_out = ssm_out.reshape(tokens, channels)
+    squares = lax.psum(jnp.sum(ssm_out * ssm_out, axis=1), ("seq", "tensor"))
+    gain = lax.dynamic_slice_in_dim(norm_gain, channel_at, channels)
+    gained = (ssm_out * gain).astype(jnp.bfloat16)
+    every = lax.all_gather(gained, "seq")
+    partial_out = sum(
+        jnp.dot(
+            every[k], w_out[k * channels : (k + 1) * channels], preferred_element_type=jnp.float32
+        )
+        for k in range(count)
+    )
+    mean_sq = squares / (HEADS * HEAD_DIM)
+    partial_out = (partial_out * lax.rsqrt(mean_sq + epsilon)[:, None]).astype(jnp.bfloat16)
+    width = w_out.shape[1]
+    by_owner = partial_out.reshape(count, ranks, own, width)
+    reduced = lax.psum_scatter(by_owner, "tensor", scatter_dimension=1, tiled=True)[:, 0]
+    final = lax.all_to_all(reduced, "seq", split_axis=0, concat_axis=0, tiled=True)
+    layer_out = final.transpose(1, 0, 2).reshape(own, count * width)
+    return (layer_out, abs_max)
+
+
 def solution(mesh):
+    blocks_of_tokens = mesh.shape["seq"]
+    heads_here = HEADS // mesh.shape["tensor"]
+    groups_here = GROUPS // mesh.shape["tensor"]
+    splits = heads_here % blocks_of_tokens == 0 and blocks_of_tokens % groups_here == 0
     return jax.shard_map(
-        local,
+        by_heads if splits else by_tokens,
         mesh=mesh,
         in_specs=(
             P(("seq", "tensor"), None),

time: 690 us -> 484 us (0.70)
  waiting for transfers between devices: 539 us -> 303 us
  blocking collectives: 77.4 us -> 98.3 us
  local copies, waits for them, and re-layouts: 4.54 us -> 21.3 us
  other arithmetic: 15.9 us -> 7.55 us
    all_gather x5 -> x2, waiting for transfers between devices: 531 us -> 48.6 us  [the longest x1 32.9 us: by_heads(): every = lax.all_gather(gained, 'seq')]
    psum x0 -> x2, waiting for transfers between devices: none -> 133 us  [the longest x1 79 us: by_heads(): bc_pre = lax.psum(bc_part, 'seq')]
    reduce_scatter x1, waiting for transfers between devices: 3.29 us -> 88.1 us  [by_heads(): x_pre = lax.psum_scatter(x_part, 'seq', scatter_dimension=0, tiled=True)[0]]
    all_gather x2 -> x0, blocking collectives: 52 us -> none  [the longest x1 32.7 us: local(): lax.all_gather(w_dt, 'seq', axis=0, tiled=True)]
    psum x1, blocking collectives: 6.21 us -> 41.9 us  [by_heads(): squares = lax.psum(jnp.sum(ssm_out * ssm_out, axis=1), ('seq', 'tensor'))]
    unnamed x6 -> x7, waiting for transfers between devices: 1.94 us -> 34 us
    pmax x1, blocking collectives: 19.2 us -> 40.4 us  [by_heads(): lax.pmax(jnp.max(jnp.abs(hidden_in.astype(jnp.float32))), ('seq', 'tensor'))]
    all_to_all x0 -> x1, blocking collectives: none -> 16 us  [by_heads(): lax.all_to_all(pieces, 'seq', split_axis=0, concat_axis=0, tiled=True)]
  transfers between devices with their start and end apart: 8 -> 7, of which waited for: 7 -> 6; matrix products, arithmetic and copies ran while one was open for 5% -> 4% of each run, Pallas kernels for 0% -> 0%
where the time goes in v1:
time: 484 us; the launch traced here: 483 us
  waiting for transfers between devices  303 us (63%)
  blocking collectives  98.3 us (20%)
  matrix products  31.7 us (7%)
  local copies, waits for them, and re-layouts  21.3 us (4%)
  between operations  15.2 us (3%)
  other arithmetic  7.55 us (2%)
  starting transfers between devices  5.76 us (1%)
    reduce_scatter x1, waiting for transfers between devices, by_heads(): x_pre = lax.psum_scatter(x_part, 'seq', scatter_dimension=0, tiled=True)[0]  88.1 us
    psum x1, waiting for transfers between devices, by_heads(): bc_pre = lax.psum(bc_part, 'seq')  79 us
    psum x1, waiting for transfers between devices, by_heads(): dt_raw = lax.psum(dt_part, 'seq')  53.7 us
    psum x1, blocking collectives, by_heads(): squares = lax.psum(jnp.sum(ssm_out * ssm_out, axis=1), ('seq', 'tensor'))  41.9 us
    pmax x1, blocking collectives, by_heads(): lax.pmax(jnp.max(jnp.abs(hidden_in.astype(jnp.float32))), ('seq', 'tensor'))  40.4 us
    unnamed x7, waiting for transfers between devices  34 us
    all_gather x1, waiting for transfers between devices, by_heads(): every = lax.all_gather(gained, 'seq')  32.9 us
    dot_general x10, matrix products, project(): return jnp.dot(quant, weight, preferred_element_type=jnp.float32) * in_scale  20.2 us
  transfers between devices with their start and end apart: 7, of which 6 were waited for; matrix products, arithmetic and copies ran while one was open for 4% of the time, Pallas kernels for 0%

profile of v1, /device:TPU:0, one launch (start us, length us, event | category | flops | bytes accessed | tf_op | source)
XLA Modules:
  0.0 483.4 jit_solution(6907678490410389006)
XLA Ops:
  8.0 1.6 fusion.36
  9.8 16.0 %all_to_all.10 = bf16[8,32,512]{2,1,0:T(8,128)(2,1)S(1)} all-to-all(bf16[8,32,512]{2,1,0:T(8,128)(2,1)S(1)} %copy.79), channel_id=1, replica_groups=mesh['seq'=8,'tensor'=4] {'seq'}, dimensions={0} | all-to-all | bytes 524288 | tf_op jit(solution)/shard_map/all_to_all | solution.py:204
  26.9 15.6 %all-gather.6.cloned.1.call-done = bf16[8,128,512]{2,0,1:T(8,128)(2,1)} async-done(((bf16[8,32,512]{2,0,1:T(8,128)(2,1)}), bf16[8,128,512]{2,0,1:T(8,128)(2,1)}) %all-gather.6.cloned.1.call-update) | async-done | bytes 1048592 | tf_op jit(solution)/shard_map/all_gather | solution.py:205
  42.6 1.5 copy.81
  44.1 2.2 fusion.26
  46.3 2.2 fusion.24
  48.5 2.2 fusion.22
  50.7 1.1 convolution_multiply_fusion.9
  51.8 1.7 multiply_convert_fusion.2
  53.5 2.2 fusion.20
  55.8 2.2 fusion.18
  58.0 2.2 fusion.16
  60.1 2.2 fusion.14
  62.4 2.2 fusion.12
  67.9 53.7 %all-reduce.7.cloned.1.call-done = f32[1024,32]{0,1:T(8,128)} async-done(((f32[1024,32]{0,1:T(8,128)}), f32[1024,32]{0,1:T(8,128)}) %all-reduce.7.cloned.1.call-update) | async-done | bytes 131088 | tf_op jit(solution)/shard_map/psum | solution.py:224
  124.0 79.0 %all-reduce.5.cloned.1.call-done = bf16[1024,512]{1,0:T(8,128)(2,1)} async-done(((bf16[1024,512]{1,0:T(8,128)(2,1)}), bf16[1024,512]{1,0:T(8,128)(2,1)}) %all-reduce.5.cloned.1.call-update) | async-done | bytes 1048592 | tf_op jit(solution)/shard_map/psum | solution.py:222
  203.0 1.1 constant_dynamic-slice_fusion.3
  204.8 1.1 fusion.76
  205.9 88.1 %reduce-scatter.5.cloned.1.call-done = bf16[1,1024,256]{2,1,0:T(8,128)(2,1)} async-done(((bf16[8,1024,256]{2,1,0:T(8,128)(2,1)}), bf16[1,1024,256]{2,1,0:T(8,128)(2,1)}) %reduce-scatter.5.cloned.1.call-update) | async-done | bytes 524304 | tf_op jit(solution)/shard_map/reduce_scatter | solution.py:220
  294.1 2.4 multiply_convert_fusion.6
  297.8 6.2 %while.12 = (s32[]{:T(128)}, f32[4,64,128]{2,1,0:T(8,128)S(1)}, f32[8,4,64,128]{3,2,1,0:T(8,128)}, f32[8,4]{1,0:T(8,128)S(1)}, f32[8,4,64,128]{3,2,1,0:T(8,128)S(1)}, /*index=5*/s32[]{:T(128)}) while((s32[]{:T(128)}, f32[4,64,128]{2,1,0:T(8,128)S(1)}, f32[8,4,64,128]{3,2,1,0:T(8,128)}, f32[8,4]{1,0:T(8,128)S(1)}, ...), condition=%wide.region_5.6_spmd, body=%wide.region_4.5_spmd.sunk | while | flops 65538 | bytes 655997 | solution.py:272
  304.0 2.0 convolution_bitcast_fusion
  308.6 2.2 copy.96
  310.9 41.9 %psum.23 = f32[1024]{0:T(1024)S(1)} all-reduce(f32[1024]{0:T(1024)S(1)} %bitcast.168), channel_id=1, replica_groups=mesh['seq'=8,'tensor'=4] {'seq','tensor'}, use_global_device_ids=true, to_apply=%region_7.8 | all-reduce | flops 1024 | bytes 8192 | tf_op jit(solution)/shard_map/psum | solution.py:281
  352.7 32.9 %all-gather.4.cloned.1.call-done = bf16[8,1024,256]{2,1,0:T(8,128)(2,1)} async-done(((bf16[1,1024,256]{2,1,0:T(8,128)(2,1)}), bf16[8,1024,256]{2,1,0:T(8,128)(2,1)}) %all-gather.4.cloned.1.call-update) | async-done | bytes 4194320 | tf_op jit(solution)/shard_map/all_gather | solution.py:284
  385.7 1.7 fusion.43
  387.4 1.5 fusion.44
  391.1 1.9 multiply_convert_fusion
  393.6 33.9 %all-reduce.9.cloned.1.call-done = bf16[8,4,32,512]{3,2,1,0:T(8,128)(2,1)} async-done(((bf16[8,4,32,512]{3,2,1,0:T(8,128)(2,1)}), bf16[8,4,32,512]{3,2,1,0:T(8,128)(2,1)}) %all-reduce.9.cloned.1.call-update) | async-done | bytes 1048592
  427.5 2.3 dynamic-slice_bitcast_fusion
  429.9 5.5 %all-to-all-start.1 = ((bf16[8,32,512]{2,1,0:T(8,128)(2,1)}), bf16[8,32,512]{2,1,0:T(8,128)(2,1)S(1)}, u32[]{:S(2)}, u32[]{:S(2)}) async-start(bf16[8,32,512]{2,1,0:T(8,128)(2,1)} %dynamic-slice_bitcast_fusion), calls=%async_computation.2 | async-start | bytes 524288 | tf_op jit(solution)/shard_map/all_to_all | solution.py:296
  435.4 40.4 %pmax.7 = f32[]{:T(128)} all-reduce(f32[]{:T(128)} %get-tuple-element.69), channel_id=1, replica_groups=mesh['seq'=8,'tensor'=4] {'seq','tensor'}, use_global_device_ids=true, to_apply=%region_10.11 | all-reduce | flops 1 | bytes 8 | tf_op jit(solution)/shard_map/pmax | solution.py:196
  (108 shorter events, 21.3 us)
Async XLA Ops:
  7.2 60.7 %copy-start = (f32[32,64,128]{2,1,0:T(8,128)S(1)}, f32[32,64,128]{2,1,0:T(8,128)}, u32[]{:S(2)}) copy-start(f32[32,64,128]{2,1,0:T(8,128)} %param.29) | copy-start | bytes 3145732
  7.2 19.6 %copy-start.4 = (bf16[512,2,2,128]{3,2,1,0:T(2,128)(2,1)S(1)}, bf16[512,2,2,128]{3,2,1,0:T(2,128)(2,1)}, u32[]{:S(2)}) copy-start(bf16[512,2,2,128]{3,2,1,0:T(2,128)(2,1)} %param.20) | copy-start | bytes 1572868
  7.2 35.4 %all-gather.6.cloned.1.call-start = ((), (), s32[]{:S(2)}) async-start(), calls=%async_computation.7 | async-start | bytes 1310720 | tf_op jit(solution)/shard_map/all_gather | solution.py:205
  26.7 95.0 %all-reduce.7.cloned.1.call-start = ((), (), s32[]{:S(2)}) async-start(), calls=%async_computation.5 | async-start | bytes 262144 | tf_op jit(solution)/shard_map/psum | solution.py:224
  46.3 4.4 copy-start.5
  51.8 151.2 %all-reduce.5.cloned.1.call-start = ((), (), s32[]{:S(2)}) async-start(), calls=%async_computation.4 | async-start | bytes 2097152 | tf_op jit(solution)/shard_map/psum | solution.py:222
  55.7 238.3 %reduce-scatter.5.cloned.1.call-start = ((), (), s32[]{:S(2)}) async-start(), calls=%async_computation.3 | async-start | bytes 4718592 | tf_op jit(solution)/shard_map/reduce_scatter | solution.py:220
  64.5 0.7 copy-start.6
  64.5 0.7 copy-start.8
  64.5 0.8 copy-start.9
  64.5 0.9 copy-start.7
  64.5 0.9 copy-start.10
  64.6 321.1 %all-gather.4.cloned.1.call-start = ((), (), s32[]{:S(2)}) async-start(), calls=%async_computation.6 | async-start | bytes 4718592 | tf_op jit(solution)/shard_map/all_gather | solution.py:284
  304.0 2.0 copy-start.3
  308.6 78.8 %copy-start.2 = (bf16[2048,512]{1,0:T(8,128)(2,1)S(1)}, bf16[2048,512]{1,0:T(8,128)(2,1)}, u32[]{:S(2)}) copy-start(bf16[2048,512]{1,0:T(8,128)(2,1)} %param.31) | copy-start | bytes 6291460
  310.8 116.7 %all-reduce.9.cloned.1.call-start = ((), (), s32[]{:S(2)}) async-start(), calls=%async_computation.8 | async-start | bytes 2097152
  385.7 3.2 copy-start.1
  391.0 1.9 copy-start.11
  429.9 45.9 %all-to-all-start.1 = ((bf16[8,32,512]{2,1,0:T(8,128)(2,1)}), bf16[8,32,512]{2,1,0:T(8,128)(2,1)S(1)}, u32[]{:S(2)}, u32[]{:S(2)}) async-start(bf16[8,32,512]{2,1,0:T(8,128)(2,1)} %dynamic-slice_bitcast_fusion), calls=%async_computation.2 | async-start | bytes 524288 | tf_op jit(solution)/shard_map/all_to_all | solution.py:296
Sparse Core Ops, SparseCore 0:
  26.8 15.7 all-gather.5
  51.9 69.7 all-reduce.6
  125.6 77.3 all-reduce.4
  206.5 87.4 reduce-scatter.4
  310.9 74.6 all-gather.3
  393.1 34.4 all-reduce.8
